TPU v7x, 512 devices: a whole 4x8x8 slice. The times are simulated.
512 devices in a mesh: dp: 32 (over x, z), vocab: 16 (over y, core).
Axes of the slice: x: 4, y: 8, z: 8, core: 2. Of those that a mesh axis runs over, the one named last changes fastest.
Arguments:
- counts: int32 [32, 16, 32, 128, 128], P('dp', 'vocab'), may hold values from 0 to 5
- tile_doc: int32 [32, 16, 32], P('dp', 'vocab'), may hold values from 0 to 3, as said below
- tile_word: int32 [32, 16, 32], P('dp', 'vocab'), may hold values from 0 to 7, as said below
- tile_live: int32 [32, 16], P('dp', 'vocab'), may hold values from 1 to 32, as said below
- doc_init: float32 [16384, 512], P('dp'), may hold values from 0.5 to 20
- topic_word: float32 [16384, 512], P(('vocab', 'dp')), may hold values from 0.01 to 10
- topic_mass: float32 [512], replicated, may hold values from 20000 to 24000
- noise: float32 [16384, 512], P(('vocab', 'dp')), may hold values from -4 to 4
Outputs:
- doc_topic: float32 [16384, 512], P(('dp', 'vocab'))
- new_topic_word: float32 [16384, 512], P(('vocab', 'dp'))
Inputs may be any that keep to these rules, and one draw needn't show every extreme that they name: `tile_doc`: the 32 slots of a device name every pair of a doc block and a word block exactly once, together with tile_word. `tile_word`: the 32 slots of a device name every pair of a doc block and a word block exactly once, together with tile_doc. Only the first tile_live slots of a device hold tiles; some device has all 32 slots live.
All inputs are finite; a program needn't handle non-finite values.
Results may differ from a plain program's by a relative error of at most 0.00065.
Values may be sent and summed in bfloat16 or wider, within the bound.
A program may use at most 64 MiB of HBM per device.

v0:
```python
import jax
import jax.numpy as jnp
from jax import lax
from jax.sharding import PartitionSpec as P

ITERS = 3


ALPHA_PRIOR = 0.1
BETA_PRIOR = 0.01
HALF_STEP = 0.05
GRAD_SCALE = 16.0


def shards(counts, tile_doc, tile_word, tile_live, doc_init, topic_word, topic_mass, noise):
    topic_count = topic_mass.shape[0]
    block_len = counts.shape[-1]
    doc_blocks = doc_init.shape[0] // block_len
    tile_counts = counts[0, 0]
    doc_pick = tile_doc[0, 0]
    word_pick = tile_word[0, 0]
    live_count = tile_live[0, 0]
    topic_prob = topic_word / topic_mass[None, :]
    panel_rows = lax.all_gather(topic_prob.astype(jnp.bfloat16), "dp", axis=0, tiled=True)
    word_blocks = panel_rows.shape[0] // block_len
    prob_blocks = panel_rows.reshape(word_blocks, block_len, topic_count)

    def tile_ratios(slot_index, doc_rows, word_rows):
        counts_here = lax.dynamic_index_in_dim(tile_counts, slot_index, 0, keepdims=False)
        rates = jnp.dot(doc_rows, word_rows.T, preferred_element_type=jnp.float32)
        return (counts_here.astype(jnp.float32) / rates).astype(jnp.bfloat16)

    vocab_index = lax.axis_index("vocab")
    share_rows = doc_init.shape[0] // lax.axis_size("vocab")
    doc_gamma = doc_init
    for iteration in range(ITERS):
        gamma_blocks = doc_gamma.astype(jnp.bfloat16).reshape(doc_blocks, block_len, topic_count)

        def doc_add_tile(slot_index, running):
            doc_index = doc_pick[slot_index]
            doc_rows = lax.dynamic_index_in_dim(gamma_blocks, doc_index, 0, keepdims=False)
            word_rows = lax.dynamic_index_in_dim(
                prob_blocks, word_pick[slot_index], 0, keepdims=False
            )
            ratios = tile_ratios(slot_index, doc_rows, word_rows)
            partial_value = jnp.dot(ratios, word_rows, preferred_element_type=jnp.float32)
            current = lax.dynamic_index_in_dim(running, doc_index, 0, keepdims=False)
            return lax.dynamic_update_index_in_dim(running, current + partial_value, doc_index, 0)

        doc_start = jnp.zeros((doc_blocks, block_len, topic_count), jnp.float32)
        partial_sums = lax.fori_loop(0, live_count, doc_add_tile, doc_start).reshape(
            -1, topic_count
        )
        summed = lax.psum(partial_sums, "vocab")
        doc_gamma = ALPHA_PRIOR + doc_gamma * summed
    gamma_bf = doc_gamma.astype(jnp.bfloat16)
    doc_share = lax.dynamic_slice_in_dim(doc_gamma, vocab_index * share_rows, share_rows, 0)
    totals = lax.psum(jnp.sum(doc_gamma - ALPHA_PRIOR, axis=0), "dp")
    word_gamma_blocks = gamma_bf.reshape(doc_blocks, block_len, topic_count)

    def word_add_tile(slot_index, running):
        word_index = word_pick[slot_index]
        doc_rows = lax.dynamic_index_in_dim(
            word_gamma_blocks, doc_pick[slot_index], 0, keepdims=False
        )
        word_rows = lax.dynamic_index_in_dim(prob_blocks, word_index, 0, keepdims=False)
        ratios = tile_ratios(slot_index, doc_rows, word_rows)
        partial_value = jnp.einsum(
            "dw,dk->wk", ratios, doc_rows, preferred_element_type=jnp.float32
        )
        current = lax.dynamic_index_in_dim(running, word_index, 0, keepdims=False)
        return lax.dynamic_update_index_in_dim(running, current + partial_value, word_index, 0)

    start = jnp.zeros((word_blocks, block_len, topic_count), jnp.float32)
    word_hits = lax.fori_loop(0, live_count, word_add_tile, start).reshape(-1, topic_count)
    reduced = lax.psum_scatter(word_hits, "dp", scatter_dimension=0, tiled=True)
    drift_term = (
        BETA_PRIOR - topic_word + GRAD_SCALE * (topic_prob * reduced - totals[None, :] * topic_prob)
    )
    updated = jnp.abs(topic_word + HALF_STEP * drift_term + jnp.sqrt(topic_word) * noise)
    doc_topic = doc_share / (jnp.sum(doc_share, axis=1, keepdims=True) / topic_count)
    return (doc_topic, updated)


def solution(mesh):
    return jax.shard_map(
        shards,
        mesh=mesh,
        in_specs=(
            P("dp", "vocab", None, None, None),
            P("dp", "vocab", None),
            P("dp", "vocab", None),
            P("dp", "vocab"),
            P("dp", None),
            P(("vocab", "dp"), None),
            P(),
            P(("vocab", "dp"), None),
        ),
        out_specs=(P(("dp", "vocab"), None), P(("vocab", "dp"), None)),
        check_vma=False,
    )
```

profile of v0, /device:TPU:1, one launch (start us, length us, event | category | flops | bytes accessed | tf_op | source)
XLA Modules:
  0.0 1578.1 jit_solution(10045171930323271985)
XLA Ops:
  7.2 1.5 divide_convert_fusion
  10.1 85.0 %all-gather.2.cloned.1.call-done = bf16[1024,512]{1,0:T(8,128)(2,1)} async-done(((bf16[32,512]{1,0:T(8,128)(2,1)}), bf16[1024,512]{1,0:T(8,128)(2,1)}) %all-gather.2.cloned.1.call-update) | async-done | bytes 1048592 | tf_op jit(solution)/shard_map/all_gather | solution.py:24
  95.2 136.7 %while.40 = (s32[]{:T(128)}, f32[4,128,512]{2,1,0:T(8,128)S(1)}, s32[]{:T(128)}, s32[32]{0:T(128)S(1)}, s32[32,128,128]{2,1,0:T(8,128)}, /*index=5*/bf16[4,128,5...) while((s32[]{:T(128)}, f32[4,128,512]{2,1,0:T(8,128)S(1)}, ...), condition=%wide.region_1.2_spmd, body=%wide.region_0.1_spmd.sunk | while | flops 33669128 | bytes 1510151 | solution.py:51
  108.2 1.4 fusion.86
  151.2 1.4 fusion.86
  158.3 1.4 fusion.86
  165.5 1.4 fusion.86
  172.6 1.4 fusion.86
  179.8 1.4 fusion.86
  187.0 1.4 fusion.86
  194.1 1.4 fusion.86
  201.3 1.4 fusion.86
  208.4 1.4 fusion.86
  215.6 1.4 fusion.86
  222.7 1.4 fusion.86
  229.9 1.4 fusion.86
  233.0 207.1 %all-reduce.4.cloned.1.call-done = f32[512,512]{1,0:T(8,128)} async-done(((f32[512,512]{1,0:T(8,128)}), f32[512,512]{1,0:T(8,128)}) %all-reduce.4.cloned.1.call-update) | async-done | bytes 1048592 | tf_op jit(solution)/shard_map/psum | solution.py:54
  440.1 2.3 fusion.64
  442.5 134.8 %while.41 = (s32[]{:T(128)}, f32[4,128,512]{2,1,0:T(8,128)S(1)}, s32[]{:T(128)}, s32[32]{0:T(128)S(1)}, s32[32,128,128]{2,1,0:T(8,128)}, /*index=5*/bf16[4,128,5...) while((s32[]{:T(128)}, f32[4,128,512]{2,1,0:T(8,128)S(1)}, ...), condition=%wide.region_4.5_spmd, body=%wide.region_3.4_spmd.sunk | while | flops 33669128 | bytes 1510151 | solution.py:51
  578.4 202.5 %all-reduce.6.cloned.1.call-done = f32[512,512]{1,0:T(8,128)} async-done(((f32[512,512]{1,0:T(8,128)}), f32[512,512]{1,0:T(8,128)}) %all-reduce.6.cloned.1.call-update) | async-done | bytes 1048592 | tf_op jit(solution)/shard_map/psum | solution.py:54
  780.9 2.7 fusion.66
  783.8 134.8 %while.42 = (s32[]{:T(128)}, f32[4,128,512]{2,1,0:T(8,128)S(1)}, s32[]{:T(128)}, s32[32]{0:T(128)S(1)}, s32[32,128,128]{2,1,0:T(8,128)}, /*index=5*/bf16[4,128,5...) while((s32[]{:T(128)}, f32[4,128,512]{2,1,0:T(8,128)S(1)}, ...), condition=%wide.region_7.8_spmd, body=%wide.region_6.7_spmd.sunk | while | flops 33669128 | bytes 1510151 | solution.py:51
  919.7 202.6 %all-reduce.8.cloned.1.call-done = f32[512,512]{1,0:T(8,128)} async-done(((f32[512,512]{1,0:T(8,128)}), f32[512,512]{1,0:T(8,128)}) %all-reduce.8.cloned.1.call-update) | async-done | bytes 1048592 | tf_op jit(solution)/shard_map/psum | solution.py:54
  1122.2 2.6 fusion.65
  1125.0 138.0 %while.43 = (s32[]{:T(128)}, f32[8,128,512]{2,1,0:T(8,128)S(1)}, s32[]{:T(128)}, s32[32]{0:T(128)S(1)}, s32[32,128,128]{2,1,0:T(8,128)}, /*index=5*/s32[32]{0:T(...) while((s32[]{:T(128)}, f32[8,128,512]{2,1,0:T(8,128)S(1)}, ...), condition=%wide.region_11.12_spmd, body=%wide.region_10.11_spmd.sunk | while | flops 33669128 | bytes 1510151 | solution.py:75
  1130.8 1.5 fusion.98
  1138.0 1.5 fusion.98
  1145.3 1.5 fusion.98
  1152.5 1.5 fusion.98
  1159.7 1.5 fusion.98
  1167.0 1.5 fusion.98
  1174.2 1.5 fusion.98
  1181.4 1.5 fusion.98
  1188.6 1.5 fusion.98
  1195.9 1.5 fusion.98
  1203.1 1.5 fusion.98
  1210.3 1.5 fusion.98
  1217.5 1.5 fusion.98
  1224.8 1.5 fusion.98
  1232.0 1.5 fusion.98
  1239.2 1.5 fusion.98
  1246.5 1.5 fusion.98
  1253.7 1.5 fusion.98
  1260.9 1.5 fusion.98
  1265.4 103.7 %psum.31 = f32[512]{0:T(512)S(1)} all-reduce(f32[512]{0:T(512)S(1)} %get-tuple-element.246), channel_id=1, replica_groups=mesh['dp'=32,'vocab'=16] {'dp'}, use_global_device_ids=true, to_apply=%region_14.15 | all-reduce | flops 512 | bytes 4096 | tf_op jit(solution)/shard_map/psum | solution.py:58
  1369.0 1.5 dynamic-slice_divide_fusion
  1370.6 199.4 %reduce-scatter.2.cloned.1.call-done = f32[32,512]{1,0:T(8,128)} async-done(((f32[1024,512]{1,0:T(8,128)}), f32[32,512]{1,0:T(8,128)}) %reduce-scatter.2.cloned.1.call-update) | async-done | bytes 65552 | tf_op jit(solution)/shard_map/reduce_scatter | solution.py:76
  1570.0 1.5 add_abs_fusion
  (311 shorter events, 156.1 us)
Async XLA Ops:
  7.2 88.0 %copy-start.10 = (s32[1,1,32]{2,1,0:T(1,128)S(1)}, s32[1,1,32]{2,1,0:T(1,128)}, u32[]{:S(2)}) copy-start(s32[1,1,32]{2,1,0:T(1,128)} %param.18) | copy-start | bytes 388
  7.2 88.0 %copy-start.9 = (s32[1,1,32]{2,1,0:T(1,128)S(1)}, s32[1,1,32]{2,1,0:T(1,128)}, u32[]{:S(2)}) copy-start(s32[1,1,32]{2,1,0:T(1,128)} %param.17) | copy-start | bytes 388
  7.2 87.9 %all-gather.2.cloned.1.call-start = ((), (), s32[]{:S(2)}) async-start(), calls=%async_computation.1 | async-start | bytes 1081344 | tf_op jit(solution)/shard_map/all_gather | solution.py:24
  8.7 431.4 %all-reduce.4.cloned.1.call-start = ((), (), s32[]{:S(2)}) async-start(), calls=%async_computation.2 | async-start | bytes 2097152 | tf_op jit(solution)/shard_map/psum | solution.py:54
  95.2 344.9 %copy-start.5 = (f32[512,512]{1,0:T(8,128)S(1)}, f32[512,512]{1,0:T(8,128)}, u32[]{:S(2)}) copy-start(f32[512,512]{1,0:T(8,128)} %param.20) | copy-start | bytes 3145732
  232.0 1.0 copy-start.2
  233.0 209.5 %copy-start = (bf16[8,128,512]{2,1,0:T(8,128)(2,1)S(1)}, bf16[8,128,512]{2,1,0:T(8,128)(2,1)}, u32[]{:S(2)}) copy-start(bf16[8,128,512]{2,1,0:T(8,128)(2,1)} %get-tuple-element.609) | copy-start | bytes 3145732
  233.0 548.0 %all-reduce.6.cloned.1.call-start = ((), (), s32[]{:S(2)}) async-start(), calls=%async_computation.3 | async-start | bytes 2097152 | tf_op jit(solution)/shard_map/psum | solution.py:54
  577.3 1.0 copy-start.3
  578.3 543.9 %all-reduce.8.cloned.1.call-start = ((), (), s32[]{:S(2)}) async-start(), calls=%async_computation.4 | async-start | bytes 2097152 | tf_op jit(solution)/shard_map/psum | solution.py:54
  918.6 1.0 copy-start.4
  919.6 650.4 %reduce-scatter.2.cloned.1.call-start = ((), (), s32[]{:S(2)}) async-start(), calls=%async_computation.5 | async-start | bytes 2162688 | tf_op jit(solution)/shard_map/reduce_scatter | solution.py:76
  1263.0 1.3 copy-start.1
  1263.0 307.0 %copy-start.6 = (f32[32,512]{1,0:T(8,128)S(1)}, f32[32,512]{1,0:T(8,128)}, u32[]{:S(2)}) copy-start(f32[32,512]{1,0:T(8,128)} %param.21) | copy-start | bytes 196612
  1263.1 306.9 %copy-start.7 = (f32[32,512]{1,0:T(8,128)S(1)}, f32[32,512]{1,0:T(8,128)}, u32[]{:S(2)}) copy-start(f32[32,512]{1,0:T(8,128)} %param.23) | copy-start | bytes 196612
  1263.1 306.9 %copy-start.8 = (f32[512]{0:T(512)S(1)}, f32[512]{0:T(512)}, u32[]{:S(2)}) copy-start(f32[512]{0:T(512)} %param.22) | copy-start | bytes 6148
Sparse Core Ops, SparseCore 0:
  11.8 83.2 all-gather.1
  233.1 206.9 all-reduce.3
  578.5 202.4 all-reduce.5
  919.7 202.4 all-reduce.7
  1264.5 305.4 reduce-scatter.1
where the time goes:
time: 1590 us; the launch traced here: 1580 us
  waiting for transfers between devices  897 us (56%)
  loops' own time  350 us (22%)
  blocking collectives  104 us (7%)
  matrix products  103 us (6%)
  local copies, waits for them, and re-layouts  96.2 us (6%)
    psum x3, waiting for transfers between devices, shards(): summed = lax.psum(partial_sums, 'vocab')  612 us
    another operation x3, loops' own time, shards(): lax.fori_loop(0, live_count, doc_add_tile, doc_start)  262 us
    reduce_scatter x1, waiting for transfers between devices, shards(): reduced = lax.psum_scatter(word_hits, 'dp', scatter_dimension=0, tiled=True)  199 us
    psum x1, blocking collectives, shards(): totals = lax.psum(jnp.sum(doc_gamma - ALPHA_PRIOR, axis=0), 'dp')  104 us
    another operation x1, loops' own time, shards(): lax.fori_loop(0, live_count, word_add_tile, start).reshape(-1, topic_count)  87.5 us
    all_gather x1, waiting for transfers between devices, shards(): lax.all_gather(topic_prob.astype(jnp.bfloat16), 'dp', axis=0, tiled=True)  85 us
    dot_general x57, matrix products, doc_add_tile(): jnp.dot(ratios, word_rows, preferred_element_type=jnp.float32)  75.3 us
    dynamic_slice x57, local copies, waits for them, and re-layouts, doc_add_tile(): word_pick[slot_index]  33.6 us
  transfers between devices with their start and end apart: 5, of which 5 were waited for; matrix products, arithmetic and copies ran while one was open for 0% of the time, Pallas kernels for 0%

commit v1 on v0

v1 whole, which is shorter than its diff:
```python
import functools

import jax
import jax.numpy as jnp
from jax import lax
from jax.experimental import pallas as pl
from jax.experimental.pallas import tpu as pltpu
from jax.sharding import PartitionSpec as P

ITERS = 3
ALPHA_PRIOR = 0.1
BETA_PRIOR = 0.01
HALF_STEP = 0.05
GRAD_SCALE = 16.0
MESH = pl.DeviceIdType.MESH
CHAINS = 2
X_CHIPS = 4


def far_first(count):
    return sorted(range(1, count), key=lambda j: -min(j, count - j))


def near_first(count):
    return sorted(range(1, count), key=lambda j: min(j, count - j))


def nt_dot(a, b):
    return lax.dot_general(a, b, (((1,), (1,)), ((), ())), preferred_element_type=jnp.float32)


def tn_dot(a, b):
    return lax.dot_general(a, b, (((0,), (0,)), ((), ())), preferred_element_type=jnp.float32)


def body(
    nx, nz, ny, share,
    slot_ref, counts_hbm, doc_hbm, word_ref, mass_ref, noise_ref,
    doc_out, word_out,
    cbuf, dbuf, cnt, cnt_sib, prob, gam_b, gam_sib, gam, part, got, hits, got_x, got_z,
    tot_y, tot_c, tot_x, tot_z,
    in_sem, doc_sem, cnt_sem,
    pz_s, pz_r, px_s, px_r, pc_s, pc_r,
    s_s, s_r, g_s, g_r, gc_s, gc_r,
    hx_s, hx_r, hz_s, hz_r,
    ty_s, ty_r, tc_s, tc_r, tx_s, tx_r, tz_s, tz_r,
):
    slots, block = counts_hbm.shape[0], counts_hbm.shape[1]
    panel = prob.shape[1]
    wblocks = panel // block
    rows_x = nz * share
    sub = share // CHAINS
    dp = lax.axis_index("dp")
    vo = lax.axis_index("vocab")
    x, z = dp // nz, lax.rem(dp, nz)
    y, c = vo // 2, lax.rem(vo, 2)
    sib = 1 - c

    def at_y(j):
        return (dp, lax.rem(y + j, ny) * 2 + c)

    def at_x(j):
        return (lax.rem(x + j, nx) * nz + z, vo)

    def at_z(j):
        return (x * nz + lax.rem(z + j, nz), vo)

    at_c = (dp, y * 2 + sib)

    def remote(src, dst, s, r, to):
        return pltpu.make_async_remote_copy(
            src_ref=src, dst_ref=dst, send_sem=s, recv_sem=r, device_id=to, device_id_type=MESH
        )

    counts_in = pltpu.make_async_copy(counts_hbm, cbuf.at[pl.ds(0, slots)], in_sem)
    counts_in.start()
    doc_in = [
        pltpu.make_async_copy(
            doc_hbm.at[pl.ds((2 * q + c) * share, share)], dbuf.at[q], doc_sem.at[q]
        )
        for q in range(ny)
    ]
    for copy in doc_in:
        copy.start()

    barrier = pltpu.get_barrier_semaphore()
    peers = [at_y(j) for j in range(1, ny)] + [at_c]
    peers += [at_x(j) for j in range(1, nx)] + [at_z(j) for j in range(1, nz)]
    for to in peers:
        pl.semaphore_signal(barrier, inc=1, device_id=to, device_id_type=MESH)

    prob_own = word_ref[...] / mass_ref[...]

    def shard(jx, jz):
        row = (lax.rem(x - jx + nx, nx) * nz + lax.rem(z - jz + nz, nz)) * share
        return prob.at[c, pl.ds(pl.multiple_of(row, share), share)]

    def xblock(jx):
        row = lax.rem(x - jx + nx, nx) * rows_x
        return prob.at[c, pl.ds(pl.multiple_of(row, rows_x), rows_x)]

    def sib_xblock(jx):
        row = lax.rem(x - jx + nx, nx) * rows_x
        return prob.at[sib, pl.ds(pl.multiple_of(row, rows_x), rows_x)]

    shard(0, 0)[...] = prob_own.astype(jnp.bfloat16)
    pl.semaphore_wait(barrier, len(peers))

    pz = {j: remote(shard(0, 0), shard(0, 0), pz_s.at[j], pz_r.at[j], at_z(j)) for j in range(1, nz)}
    px = {
        (jx, jz): remote(shard(0, jz), shard(0, jz), px_s.at[jx, jz], px_r.at[jx, jz], at_x(jx))
        for jx in range(1, nx)
        for jz in range(nz)
    }
    for j in far_first(nz):
        pz[j].start()
    for jx in far_first(nx):
        px[jx, 0].start()

    counts_in.wait()
    cbuf[slots] = jnp.zeros((block, block), jnp.int32)
    per_block = block // share
    pairs = per_block // 2 if per_block > 1 else 1

    def place(t, _):
        d, w = t // wblocks, lax.rem(t, wblocks)
        slot = slot_ref[t]
        col = pl.ds(pl.multiple_of(w * block, block), block)
        for k in range(pairs):
            for other in range(2):
                core = sib if other else c
                piece = cbuf[slot, pl.ds(pl.multiple_of((2 * k + core) * share, share), share), :]
                piece = piece.astype(jnp.float32).astype(jnp.bfloat16)
                for h in range(CHAINS):
                    row = pl.ds(pl.multiple_of((d * pairs + k) * sub, sub), sub)
                    val = piece[h * sub:(h + 1) * sub]
                    if other:
                        cnt_sib[h, row, col] = val
                    else:
                        cnt[c, h, row, col] = val
        return 0

    lax.fori_loop(0, slots, place, 0)
    cnt_go = remote(cnt_sib, cnt.at[c], cnt_sem.at[0], cnt_sem.at[1], at_c)
    cnt_go.start()

    for copy in doc_in:
        copy.wait()
    for h in range(CHAINS):
        for q in range(ny):
            gam_b[h, q * sub:(q + 1) * sub, :] = dbuf[q, h * sub:(h + 1) * sub, :].astype(jnp.bfloat16)
        gam[h] = dbuf[y, h * sub:(h + 1) * sub, :]

    for jz in near_first(nz):
        remote(shard(0, jz), shard(0, jz), pz_s.at[jz], pz_r.at[jz], at_z(jz)).wait_recv()
        for jx in far_first(nx):
            px[jx, jz].start()
    pc = [remote(xblock(jx), xblock(jx), pc_s.at[jx], pc_r.at[jx], at_c) for jx in range(nx)]
    pc[0].start()
    for jx in near_first(nx):
        for jz in [0] + near_first(nz):
            remote(shard(jx, jz), shard(jx, jz), px_s.at[jx, jz], px_r.at[jx, jz], at_x(jx)).wait_recv()
        pc[jx].start()
    remote(cnt_sib, cnt.at[sib], cnt_sem.at[0], cnt_sem.at[1], at_c).wait_recv()
    for jx in range(nx):
        remote(sib_xblock(jx), sib_xblock(jx), pc_s.at[jx], pc_r.at[jx], at_c).wait_recv()

    chunk = min(512, panel)
    per_panel = panel // chunk

    def partial_sums(h):
        part[h] = jnp.zeros(part.shape[1:], jnp.float32)

        def step(t, _):
            side, k = t // per_panel, lax.rem(t, per_panel)
            words = pl.ds(pl.multiple_of(k * chunk, chunk), chunk)
            p = prob[side, words, :]
            rates = nt_dot(gam_b[h], p)
            ratios = (cnt[side, h, :, words].astype(jnp.float32) / rates).astype(jnp.bfloat16)
            part[h] += jnp.dot(ratios, p, preferred_element_type=jnp.float32)
            return 0

        lax.fori_loop(0, 2 * per_panel, step, 0)

    def doc_rows(j):
        return pl.ds(pl.multiple_of(lax.rem(y + j + ny, ny) * sub, sub), sub)

    def send_sums(h, j):
        return remote(part.at[h, doc_rows(j)], got.at[h, j], s_s.at[h, j], s_r.at[h, j], at_y(j))

    def send_gamma(h, j):
        own = gam_b.at[h, doc_rows(0)]
        return remote(own, own, g_s.at[h, j], g_r.at[h, j], at_y(j))

    def wait_gamma(h, j):
        theirs = gam_b.at[h, doc_rows(-j)]
        remote(theirs, theirs, g_s.at[h, j], g_r.at[h, j], at_y(j)).wait_recv()

    for it in range(ITERS):
        for h in range(CHAINS):
            if it:
                for j in near_first(ny):
                    wait_gamma(h, j)
                for j in range(1, ny):
                    send_sums(h, j).wait_send()
            partial_sums(h)
            for j in far_first(ny):
                send_sums(h, j).start()
        for h in range(CHAINS):
            total = part[h, doc_rows(0), :]
            for j in near_first(ny):
                send_sums(h, j).wait_recv()
                total = total + got[h, j]
            gam[h] = ALPHA_PRIOR + gam[h] * total
            if it:
                for j in range(1, ny):
                    send_gamma(h, j).wait_send()
            gam_b[h, doc_rows(0), :] = gam[h].astype(jnp.bfloat16)
            for j in far_first(ny):
                send_gamma(h, j).start()

    final = jnp.concatenate([gam[h] for h in range(CHAINS)], axis=0)
    tot_y[0] = jnp.sum(final - ALPHA_PRIOR, axis=0, keepdims=True)

    def send_ty(j):
        return remote(tot_y.at[0], tot_y.at[j], ty_s.at[j], ty_r.at[j], at_y(j))

    for j in far_first(ny):
        send_ty(j).start()
    topics = final.shape[1]
    doc_out[...] = final / (jnp.sum(final, axis=1, keepdims=True) / topics)

    def give(h):
        return remote(gam_b.at[h], gam_sib.at[h], gc_s.at[h], gc_r.at[h], at_c)

    for h in range(CHAINS):
        for j in near_first(ny):
            wait_gamma(h, j)
        give(h).start()
    total = tot_y[0]
    for j in near_first(ny):
        send_ty(j).wait_recv()
        total = total + tot_y[j]
    tot_c[0] = total
    send_tc = remote(tot_c.at[0], tot_c.at[1], tc_s, tc_r, at_c)
    send_tc.start()
    for h in range(CHAINS):
        give(h).wait_recv()
    send_tc.wait_recv()
    tot_x[0] = tot_c[0] + tot_c[1]

    def send_tx(j):
        return remote(tot_x.at[0], tot_x.at[j], tx_s.at[j], tx_r.at[j], at_x(j))

    for j in far_first(nx):
        send_tx(j).start()

    def send_hx(j):
        return remote(hits.at[j], got_x.at[j], hx_s.at[j], hx_r.at[j], at_x(j))

    for j in far_first(nx) + [0]:
        words = pl.ds(pl.multiple_of(lax.rem(x + j, nx) * rows_x, rows_x), rows_x)
        p = prob[c, words, :]
        for h in range(CHAINS):
            for other in range(2):
                g = gam_sib[h] if other else gam_b[h]
                n = cnt_sib[h, :, words] if other else cnt[c, h, :, words]
                ratios = (n.astype(jnp.float32) / nt_dot(g, p)).astype(jnp.bfloat16)
                add = tn_dot(ratios, g)
                if h == 0 and other == 0:
                    hits[j] = add
                else:
                    hits[j] += add
        if j:
            send_hx(j).start()

    total = tot_x[0]
    for j in near_first(nx):
        send_tx(j).wait_recv()
        total = total + tot_x[j]
    tot_z[0] = total

    def send_tz(j):
        return remote(tot_z.at[0], tot_z.at[j], tz_s.at[j], tz_r.at[j], at_z(j))

    for j in far_first(nz):
        send_tz(j).start()
    for j in near_first(nx):
        send_hx(j).wait_recv()

    def z_rows(j):
        return pl.ds(pl.multiple_of(lax.rem(z + j, nz) * share, share), share)

    def send_hz(j):
        return remote(hits.at[0, z_rows(j)], got_z.at[j], hz_s.at[j], hz_r.at[j], at_z(j))

    for j in far_first(nz) + [0]:
        total = hits[0, z_rows(j), :]
        for jx in range(1, nx):
            total = total + got_x[jx, z_rows(j), :]
        hits[0, z_rows(j), :] = total
        if j:
            send_hz(j).start()

    total = tot_z[0]
    for j in near_first(nz):
        send_tz(j).wait_recv()
        total = total + tot_z[j]
    totals = total
    reduced = hits[0, z_rows(0), :]
    for j in near_first(nz):
        send_hz(j).wait_recv()
        reduced = reduced + got_z[j]
    word = word_ref[...]
    probs = word / mass_ref[...]
    drift = BETA_PRIOR - word + GRAD_SCALE * (probs * reduced - totals * probs)
    word_out[...] = jnp.abs(word + HALF_STEP * drift + jnp.sqrt(word) * noise_ref[...])

    for j in range(1, nz):
        pz[j].wait_send()
        send_hz(j).wait_send()
        send_tz(j).wait_send()
    for jx in range(1, nx):
        send_hx(jx).wait_send()
        send_tx(jx).wait_send()
        for jz in range(nz):
            px[jx, jz].wait_send()
    for jx in range(nx):
        pc[jx].wait_send()
    cnt_go.wait_send()
    send_tc.wait_send()
    for h in range(CHAINS):
        give(h).wait_send()
        for j in range(1, ny):
            send_sums(h, j).wait_send()
            send_gamma(h, j).wait_send()
    for j in range(1, ny):
        send_ty(j).wait_send()


def shards(counts, tile_doc, tile_word, tile_live, doc_init, topic_word, topic_mass, noise):
    topics = topic_mass.shape[0]
    slots, block = counts.shape[2], counts.shape[3]
    n_dp, n_vocab = lax.axis_size("dp"), lax.axis_size("vocab")
    nx = X_CHIPS
    nz, ny = n_dp // nx, n_vocab // 2
    share = topic_word.shape[0]
    panel = share * n_dp
    sub = share // CHAINS
    docs = ny * sub
    wblocks = panel // block

    order = jnp.arange(slots, dtype=jnp.int32)
    key = tile_doc[0, 0] * wblocks + tile_word[0, 0]
    usable = jnp.where(order < tile_live[0, 0], order, slots)
    slot_of = jnp.sum(jnp.where(key[None, :] == order[:, None], usable[None, :], 0), axis=1)

    f32, bf16, dma = jnp.float32, jnp.bfloat16, pltpu.SemaphoreType.DMA
    vmem = pl.BlockSpec(memory_space=pltpu.VMEM)
    return pl.pallas_call(
        functools.partial(body, nx, nz, ny, share),
        out_shape=(
            jax.ShapeDtypeStruct((share, topics), f32),
            jax.ShapeDtypeStruct((share, topics), f32),
        ),
        in_specs=[
            pl.BlockSpec(memory_space=pltpu.SMEM),
            pl.BlockSpec(memory_space=pl.ANY),
            pl.BlockSpec(memory_space=pl.ANY),
            vmem, vmem, vmem,
        ],
        out_specs=(vmem, vmem),
        scratch_shapes=[
            pltpu.VMEM((slots + 1, block, block), jnp.int32),
            pltpu.VMEM((ny, share, topics), f32),
            pltpu.VMEM((2, CHAINS, docs, panel), bf16),
            pltpu.VMEM((CHAINS, docs, panel), bf16),
            pltpu.VMEM((2, panel, topics), bf16),
            pltpu.VMEM((CHAINS, docs, topics), bf16),
            pltpu.VMEM((CHAINS, docs, topics), bf16),
            pltpu.VMEM((CHAINS, sub, topics), f32),
            pltpu.VMEM((CHAINS, docs, topics), f32),
            pltpu.VMEM((CHAINS, ny, sub, topics), f32),
            pltpu.VMEM((nx, nz * share, topics), f32),
            pltpu.VMEM((nx, nz * share, topics), f32),
            pltpu.VMEM((nz, share, topics), f32),
            pltpu.VMEM((ny, 1, topics), f32),
            pltpu.VMEM((2, 1, topics), f32),
            pltpu.VMEM((nx, 1, topics), f32),
            pltpu.VMEM((nz, 1, topics), f32),
            dma, dma((ny,)), dma((2,)),
            dma((nz,)), dma((nz,)), dma((nx, nz)), dma((nx, nz)), dma((nx,)), dma((nx,)),
            dma((CHAINS, ny)), dma((CHAINS, ny)), dma((CHAINS, ny)), dma((CHAINS, ny)),
            dma((CHAINS,)), dma((CHAINS,)),
            dma((nx,)), dma((nx,)), dma((nz,)), dma((nz,)),
            dma((ny,)), dma((ny,)), dma, dma, dma((nx,)), dma((nx,)), dma((nz,)), dma((nz,)),
        ],
        compiler_params=pltpu.CompilerParams(
            collective_id=0, has_side_effects=True, vmem_limit_bytes=48 * 2**20
        ),
    )(slot_of, counts[0, 0], doc_init, topic_word, topic_mass[None, :], noise)


def solution(mesh):
    return jax.shard_map(
        shards,
        mesh=mesh,
        in_specs=(
            P("dp", "vocab", None, None, None),
            P("dp", "vocab", None),
            P("dp", "vocab", None),
            P("dp", "vocab"),
            P("dp", None),
            P(("vocab", "dp"), None),
            P(),
            P(("vocab", "dp"), None),
        ),
        out_specs=(P(("dp", "vocab"), None), P(("vocab", "dp"), None)),
        check_vma=False,
    )
```

time: 1590 us -> 147 us (0.09)
  waiting for transfers between devices: 897 us -> 0 us
  loops' own time: 350 us -> 0 us
  Pallas kernels: 0 us -> 139 us
  blocking collectives: 104 us -> 0 us
  matrix products: 103 us -> 0 us
  local copies, waits for them, and re-layouts: 96.2 us -> 6.43 us
    psum x3 -> x0, waiting for transfers between devices: 612 us -> none  [shards(): summed = lax.psum(partial_sums, 'vocab')]
    another operation x4 -> x0, loops' own time: 350 us -> none  [the longest x3 262 us: shards(): lax.fori_loop(0, live_count, doc_add_tile, doc_start)]
    reduce_scatter x1 -> x0, waiting for transfers between devices: 199 us -> none  [shards(): reduced = lax.psum_scatter(word_hits, 'dp', scatter_dimension=0, tiled=True)]
    pallas_call x0 -> x1, Pallas kernels: none -> 139 us  [shards(): pl.pallas_call(functools.partial(body, nx, nz, ny, share), out_shape=(jax...]
    psum x1 -> x0, blocking collectives: 104 us -> none  [shards(): totals = lax.psum(jnp.sum(doc_gamma - ALPHA_PRIOR, axis=0), 'dp')]
    dot_general x76 -> x0, matrix products: 103 us -> none  [the longest x57 75.3 us: doc_add_tile(): jnp.dot(ratios, word_rows, preferred_element_type=jnp.float32)]
    dynamic_slice x228 -> x0, local copies, waits for them, and re-layouts: 91.4 us -> none  [the longest x57 33.6 us: doc_add_tile(): word_pick[slot_index]]
    all_gather x1 -> x0, waiting for transfers between devices: 85 us -> none  [shards(): lax.all_gather(topic_prob.astype(jnp.bfloat16), 'dp', axis=0, tiled=True)]
  transfers between devices with their start and end apart: 5 -> 0, of which waited for: 5 -> 0; matrix products, arithmetic and copies ran while one was open for 0% -> 0% of each run, Pallas kernels for 0% -> 0%
where the time goes in v1:
time: 147 us
  Pallas kernels  139 us (95%)
  local copies, waits for them, and re-layouts  6.43 us (4%)
    pallas_call x1, Pallas kernels, shards(): pl.pallas_call(functools.partial(body, nx, nz, ny, share), out_shape=(jax...  139 us
    unnamed x12, local copies, waits for them, and re-layouts  6.43 us

profile of v1, /device:TPU:1, one launch (start us, length us, event | category | flops | bytes accessed | tf_op | source)
XLA Modules:
  0.0 147.1 jit_solution(13536342220310846768)
XLA Ops:
  1.3 0.7 add_bitcast_fusion
  2.0 0.1 select_reduce_fusion.slot_ref
  2.1 0.0 copy-start
  2.1 1.6 %copy-done = s32[1,1,32,128,128]{4,3,2,1,0:T(8,128)S(1)} copy-done((s32[1,1,32,128,128]{4,3,2,1,0:T(8,128)S(1)}, s32[1,1,32,128,128]{4,3,2,1,0:T(8,128)}, u32[]{:S(2)}) %copy-start) | copy-done | bytes 2097176
  3.7 0.0 copy-start.1
  3.7 1.2 copy-done.1
  4.9 0.0 copy-start.2
  4.9 0.8 copy-done.2
  5.7 0.0 copy-start.3
  5.7 0.8 copy-done.3
  6.6 0.0 copy-start.4
  6.6 0.7 copy-done.4
  7.3 138.5 %shard_map.95 = (f32[32,512]{1,0:T(8,128)S(1)}, f32[32,512]{1,0:T(8,128)S(1)}) custom-call(s32[32]{0:T(128)S(1)} %select_reduce_fusion.slot_ref, s32[32,128,128]{2,1,0:T(8,128)S(1)} %bitcast.6, f32[512,512]{1,0:T(8,128)S(1)} %copy-done.1, f32[32,512]{1,0:T(8,128)S(1)} %copy-done.2, f32[1,512]{1,0:T(1,128)S(1)} %bitcast.7, f32[32,512]{1,0:T(8,128)S(1)} %copy-done.3), custom_call_target="tpu_custom_call" | custom-call | tf_op jit(solution)/shard_map/pallas_call | solution.py:360
  145.8 0.6 copy.13
  146.4 0.6 copy.14
  (1 shorter events, 0.0 us)
Async XLA Ops:
  2.1 1.6 %copy-start = (s32[1,1,32,128,128]{4,3,2,1,0:T(8,128)S(1)}, s32[1,1,32,128,128]{4,3,2,1,0:T(8,128)}, u32[]{:S(2)}) copy-start(s32[1,1,32,128,128]{4,3,2,1,0:T(8,128)} %param.8) | copy-start | bytes 6291460
  3.7 1.2 copy-start.1
  4.9 0.8 copy-start.2
  5.7 0.8 copy-start.3
  6.6 0.7 copy-start.4

commit v2 on v1

v2 whole, which is shorter than its diff:
```python
import functools

import jax
import jax.numpy as jnp
from jax import lax
from jax.experimental import pallas as pl
from jax.experimental.pallas import tpu as pltpu
from jax.sharding import PartitionSpec as P

ITERS = 3
ALPHA_PRIOR = 0.1
BETA_PRIOR = 0.01
HALF_STEP = 0.05
GRAD_SCALE = 16.0
MESH = pl.DeviceIdType.MESH
CHAINS = 2
X_CHIPS = 4
VMEM_LIMIT = 58 * 2**20


def far_first(count):
    return sorted(range(1, count), key=lambda j: -min(j, count - j))


def near_first(count):
    return sorted(range(1, count), key=lambda j: min(j, count - j))


def nt_dot(a, b):
    return lax.dot_general(a, b, (((1,), (1,)), ((), ())), preferred_element_type=jnp.float32)


def body(
    nx, nz, ny, share,
    doc_pick, word_pick, live, counts_hbm, doc_hbm, word_hbm, mass_hbm, noise_hbm,
    doc_out, word_out,
    slot_vm, slot_ref, cbuf, dbuf, word_ref, mass_ref, noise_ref,
    cnt, cnt_sib, cnt_t, prob, gall, gam, part, got, hits, got_x, got_z,
    tot_y, tot_c, tot_x, tot_z,
    in_sem, doc_sem, cnt_sem,
    pz_s, pz_r, px_s, px_r, pc_s, pc_r,
    s_s, s_r, g_s, g_r, gc_s, gc_r,
    hx_s, hx_r, hz_s, hz_r,
    ty_s, ty_r, tc_s, tc_r, tx_s, tx_r, tz_s, tz_r,
):
    slots, block = counts_hbm.shape[2], counts_hbm.shape[3]
    panel, topics = prob.shape[1], prob.shape[2]
    wblocks = panel // block
    rows_x = nz * share
    sub = share // CHAINS
    docs = ny * sub
    dp = lax.axis_index("dp")
    vo = lax.axis_index("vocab")
    x, z = dp // nz, lax.rem(dp, nz)
    y, c = vo // 2, lax.rem(vo, 2)
    sib = 1 - c

    def at_y(j):
        return (dp, lax.rem(y + j, ny) * 2 + c)

    def at_x(j):
        return (lax.rem(x + j, nx) * nz + z, vo)

    def at_z(j):
        return (x * nz + lax.rem(z + j, nz), vo)

    at_c = (dp, y * 2 + sib)

    def remote(src, dst, s, r, to):
        return pltpu.make_async_remote_copy(
            src_ref=src, dst_ref=dst, send_sem=s, recv_sem=r, device_id=to, device_id_type=MESH
        )

    word_in = pltpu.make_async_copy(word_hbm, word_ref, in_sem.at[0])
    mass_in = pltpu.make_async_copy(mass_hbm, mass_ref, in_sem.at[1])
    word_in.start()
    mass_in.start()

    barrier = pltpu.get_barrier_semaphore()
    peers = [at_y(j) for j in range(1, ny)] + [at_c]
    peers += [at_x(j) for j in range(1, nx)] + [at_z(j) for j in range(1, nz)]
    for to in peers:
        pl.semaphore_signal(barrier, inc=1, device_id=to, device_id_type=MESH)

    counts_in = pltpu.make_async_copy(counts_hbm.at[0, 0], cbuf.at[pl.ds(0, slots)], in_sem.at[2])
    counts_in.start()
    doc_in = [
        pltpu.make_async_copy(
            doc_hbm.at[pl.ds((2 * q + c) * share, share)], dbuf.at[q], doc_sem.at[q]
        )
        for q in range(ny)
    ]
    for copy in doc_in:
        copy.start()
    noise_in = pltpu.make_async_copy(noise_hbm, noise_ref, in_sem.at[3])
    noise_in.start()

    lane = lax.broadcasted_iota(jnp.int32, (1, 128), 1)
    slot_of = jnp.full((1, 128), slots, jnp.int32)
    for s in range(slots):
        key = doc_pick[0, 0, s] * wblocks + word_pick[0, 0, s]
        use = jnp.where(s < live[0, 0], s, slots)
        slot_of = jnp.where(lane == key, use, slot_of)
    slot_vm[...] = slot_of
    slot_in = pltpu.make_async_copy(slot_vm, slot_ref, in_sem.at[4])
    slot_in.start()

    def word_rows(jx, jz):
        row = (lax.rem(x - jx + nx, nx) * nz + lax.rem(z - jz + nz, nz)) * share
        return pl.ds(pl.multiple_of(row, share), share)

    def word_block(jx):
        return pl.ds(pl.multiple_of(lax.rem(x - jx + nx, nx) * rows_x, rows_x), rows_x)

    def shard(jx, jz):
        return prob.at[c, word_rows(jx, jz)]

    word_in.wait()
    mass_in.wait()
    prob[c, word_rows(0, 0), :] = (word_ref[...] / mass_ref[...]).astype(jnp.bfloat16)
    pl.semaphore_wait(barrier, len(peers))

    pz = {j: remote(shard(0, 0), shard(0, 0), pz_s.at[j], pz_r.at[j], at_z(j)) for j in range(1, nz)}
    px = {
        (jx, jz): remote(shard(0, jz), shard(0, jz), px_s.at[jx, jz], px_r.at[jx, jz], at_x(jx))
        for jx in range(1, nx)
        for jz in range(nz)
    }
    pc = [
        remote(prob.at[c, word_block(jx)], prob.at[c, word_block(jx)], pc_s.at[jx], pc_r.at[jx], at_c)
        for jx in range(nx)
    ]
    for j in near_first(nz):
        pz[j].start()
    for jx in far_first(nx):
        px[jx, 0].start()

    for copy in doc_in:
        copy.wait()
    for h in range(CHAINS):
        for q in range(ny):
            gall[q, c, h] = dbuf[q, h * sub:(h + 1) * sub, :].astype(jnp.bfloat16)
        gam[h] = dbuf[y, h * sub:(h + 1) * sub, :]

    for jz in near_first(nz):
        remote(shard(0, jz), shard(0, jz), pz_s.at[jz], pz_r.at[jz], at_z(jz)).wait_recv()
        for jx in far_first(nx):
            px[jx, jz].start()
    pc[0].start()

    counts_in.wait()
    slot_in.wait()
    cbuf[slots] = jnp.zeros((block, block), jnp.int32)
    pairs = block // share // 2

    def place(t, _):
        d, w = t // wblocks, lax.rem(t, wblocks)
        slot = slot_ref[0, t]
        col = pl.ds(pl.multiple_of(w * block, block), block)
        for k in range(pairs):
            for other in range(2):
                core = sib if other else c
                piece = cbuf[slot, pl.ds(pl.multiple_of((2 * k + core) * share, share), share), :]
                piece = piece.astype(jnp.float32).astype(jnp.bfloat16)
                for h in range(CHAINS):
                    row = pl.ds(pl.multiple_of((d * pairs + k) * sub, sub), sub)
                    val = piece[h * sub:(h + 1) * sub]
                    if other:
                        cnt_sib[h, row, col] = val
                    else:
                        cnt[c, h, row, col] = val
        return 0

    lax.fori_loop(0, slots, place, 0)
    cnt_go = remote(cnt_sib, cnt.at[c], cnt_sem.at[0], cnt_sem.at[1], at_c)
    cnt_go.start()

    def turn(w, _):
        row = pl.ds(pl.multiple_of(w * block, block), block)
        for d in range(slots // wblocks):
            tile = cbuf[slot_ref[0, d * wblocks + w]].astype(jnp.float32)
            cnt_t[row, d * block:(d + 1) * block] = tile.T.astype(jnp.bfloat16)
        return 0

    lax.fori_loop(0, wblocks, turn, 0)

    def chain_gamma(h):
        return jnp.concatenate([gall[q, c, h] for q in range(ny)], axis=0)

    both = jnp.concatenate([chain_gamma(h) for h in range(CHAINS)], axis=0)

    def first_sums(side, jx, first):
        words = word_block(jx)
        p = prob[side, words, :]
        n = jnp.concatenate([cnt[side, h, :, words] for h in range(CHAINS)], axis=0)
        ratios = (n.astype(jnp.float32) / nt_dot(both, p)).astype(jnp.bfloat16)
        add = jnp.dot(ratios, p, preferred_element_type=jnp.float32)
        for h in range(CHAINS):
            if first:
                part[h] = add[h * docs:(h + 1) * docs]
            else:
                part[h] += add[h * docs:(h + 1) * docs]

    def sib_sums(jx):
        theirs = prob.at[sib, word_block(jx)]
        remote(theirs, theirs, pc_s.at[jx], pc_r.at[jx], at_c).wait_recv()
        first_sums(sib, jx, False)

    first_sums(c, 0, True)
    remote(cnt_sib, cnt.at[sib], cnt_sem.at[0], cnt_sem.at[1], at_c).wait_recv()
    sib_sums(0)
    before = None
    for jx in near_first(nx):
        for jz in [0] + near_first(nz):
            remote(shard(jx, jz), shard(jx, jz), px_s.at[jx, jz], px_r.at[jx, jz], at_x(jx)).wait_recv()
        pc[jx].start()
        first_sums(c, jx, False)
        if before is not None:
            sib_sums(before)
        before = jx
    sib_sums(before)

    chunk = min(512, panel)

    def partial_sums(h):
        g = chain_gamma(h)
        total = None
        for side in range(2):
            for k in range(panel // chunk):
                words = pl.ds(k * chunk, chunk)
                p = prob[side, words, :]
                n = cnt[side, h, :, words].astype(jnp.float32)
                ratios = (n / nt_dot(g, p)).astype(jnp.bfloat16)
                add = jnp.dot(ratios, p, preferred_element_type=jnp.float32)
                total = add if total is None else total + add
        part[h] = total

    def doc_rows(j):
        return pl.ds(pl.multiple_of(lax.rem(y + j + ny, ny) * sub, sub), sub)

    def send_sums(h, j):
        return remote(part.at[h, doc_rows(j)], got.at[h, j], s_s.at[h, j], s_r.at[h, j], at_y(j))

    def send_gamma(h, j):
        own = gall.at[y, c, h]
        return remote(own, own, g_s.at[h, j], g_r.at[h, j], at_y(j))

    def wait_gamma(h, j):
        theirs = gall.at[lax.rem(y - j + ny, ny), c, h]
        remote(theirs, theirs, g_s.at[h, j], g_r.at[h, j], at_y(j)).wait_recv()

    for it in range(ITERS):
        for h in range(CHAINS):
            if it:
                for j in near_first(ny):
                    wait_gamma(h, j)
                for j in range(1, ny):
                    send_sums(h, j).wait_send()
                partial_sums(h)
            for j in far_first(ny):
                send_sums(h, j).start()
        for h in range(CHAINS):
            total = part[h, doc_rows(0), :]
            for j in near_first(ny):
                send_sums(h, j).wait_recv()
                total = total + got[h, j]
            gam[h] = ALPHA_PRIOR + gam[h] * total
            if it:
                for j in range(1, ny):
                    send_gamma(h, j).wait_send()
            gall[y, c, h] = gam[h].astype(jnp.bfloat16)
            for j in far_first(ny):
                send_gamma(h, j).start()

    final = jnp.concatenate([gam[h] for h in range(CHAINS)], axis=0)
    tot_y[0] = jnp.sum(final - ALPHA_PRIOR, axis=0, keepdims=True)

    def send_ty(j):
        return remote(tot_y.at[0], tot_y.at[j], ty_s.at[j], ty_r.at[j], at_y(j))

    for j in far_first(ny):
        send_ty(j).start()
    doc_out[...] = final / (jnp.sum(final, axis=1, keepdims=True) / topics)

    def give(h):
        mine = gall.at[:, c, h]
        return remote(mine, mine, gc_s.at[h], gc_r.at[h], at_c)

    def wait_give(h):
        theirs = gall.at[:, sib, h]
        remote(theirs, theirs, gc_s.at[h], gc_r.at[h], at_c).wait_recv()

    for h in range(CHAINS):
        for j in near_first(ny):
            wait_gamma(h, j)
        give(h).start()
    total = tot_y[0]
    for j in near_first(ny):
        send_ty(j).wait_recv()
        total = total + tot_y[j]
    tot_c[0] = total
    send_tc = remote(tot_c.at[0], tot_c.at[1], tc_s, tc_r, at_c)
    send_tc.start()
    for h in range(CHAINS):
        wait_give(h)

    def z_rows(j):
        return pl.ds(pl.multiple_of(lax.rem(z + j, nz) * share, share), share)

    def send_hx(jx, jz):
        return remote(
            hits.at[jx, z_rows(jz)], got_x.at[jx, z_rows(jz)],
            hx_s.at[jx, jz], hx_r.at[jx, jz], at_x(jx),
        )

    def send_hz(j):
        return remote(hits.at[0, z_rows(j)], got_z.at[j], hz_s.at[j], hz_r.at[j], at_z(j))

    def send_tx(j):
        return remote(tot_x.at[0], tot_x.at[j], tx_s.at[j], tx_r.at[j], at_x(j))

    def send_tz(j):
        return remote(tot_z.at[0], tot_z.at[j], tz_s.at[j], tz_r.at[j], at_z(j))

    gamma_all = gall[...].reshape(2 * CHAINS * docs, topics)
    z_order = far_first(nz) + [0]
    for jx in far_first(nx) + [0]:
        words = word_block(nx - jx)
        rates = nt_dot(prob[c, words, :], gamma_all)
        ratios = (cnt_t[words, :].astype(jnp.float32) / rates).astype(jnp.bfloat16)
        hits[jx] = jnp.dot(ratios, gamma_all, preferred_element_type=jnp.float32)
        if jx:
            for jz in z_order:
                send_hx(jx, jz).start()

    send_tc.wait_recv()
    tot_x[0] = tot_c[0] + tot_c[1]
    for j in far_first(nx):
        send_tx(j).start()
    total = tot_x[0]
    for j in near_first(nx):
        send_tx(j).wait_recv()
        total = total + tot_x[j]
    tot_z[0] = total
    for j in far_first(nz):
        send_tz(j).start()

    for jz in z_order:
        total = hits[0, z_rows(jz), :]
        for jx in range(1, nx):
            send_hx(jx, jz).wait_recv()
            total = total + got_x[jx, z_rows(jz), :]
        hits[0, z_rows(jz), :] = total
        if jz:
            send_hz(jz).start()

    totals = tot_z[0]
    for j in near_first(nz):
        send_tz(j).wait_recv()
        totals = totals + tot_z[j]
    noise_in.wait()
    reduced = hits[0, z_rows(0), :]
    for j in near_first(nz):
        send_hz(j).wait_recv()
        reduced = reduced + got_z[j]
    word = word_ref[...]
    probs = word / mass_ref[...]
    drift = BETA_PRIOR - word + GRAD_SCALE * (probs * reduced - totals * probs)
    word_out[...] = jnp.abs(word + HALF_STEP * drift + jnp.sqrt(word) * noise_ref[...])

    for j in range(1, nz):
        pz[j].wait_send()
        send_hz(j).wait_send()
        send_tz(j).wait_send()
    for jx in range(1, nx):
        send_tx(jx).wait_send()
        for jz in range(nz):
            px[jx, jz].wait_send()
            send_hx(jx, jz).wait_send()
    for jx in range(nx):
        pc[jx].wait_send()
    cnt_go.wait_send()
    send_tc.wait_send()
    for h in range(CHAINS):
        give(h).wait_send()
        for j in range(1, ny):
            send_sums(h, j).wait_send()
            send_gamma(h, j).wait_send()
    for j in range(1, ny):
        send_ty(j).wait_send()


def shards(counts, tile_doc, tile_word, tile_live, doc_init, topic_word, topic_mass, noise):
    topics = topic_mass.shape[0]
    slots, block = counts.shape[2], counts.shape[3]
    n_dp, n_vocab = lax.axis_size("dp"), lax.axis_size("vocab")
    nx = X_CHIPS
    nz, ny = n_dp // nx, n_vocab // 2
    share = topic_word.shape[0]
    panel = share * n_dp
    sub = share // CHAINS
    docs = ny * sub

    f32, bf16, dma = jnp.float32, jnp.bfloat16, pltpu.SemaphoreType.DMA
    vmem = pl.BlockSpec(memory_space=pltpu.VMEM)
    smem = pl.BlockSpec(memory_space=pltpu.SMEM)
    hbm = pl.BlockSpec(memory_space=pl.ANY)
    return pl.pallas_call(
        functools.partial(body, nx, nz, ny, share),
        out_shape=(
            jax.ShapeDtypeStruct((share, topics), f32),
            jax.ShapeDtypeStruct((share, topics), f32),
        ),
        in_specs=[smem, smem, smem, hbm, hbm, hbm, hbm, hbm],
        out_specs=(vmem, vmem),
        scratch_shapes=[
            pltpu.VMEM((1, 128), jnp.int32),
            pltpu.SMEM((1, 128), jnp.int32),
            pltpu.VMEM((slots + 1, block, block), jnp.int32),
            pltpu.VMEM((ny, share, topics), f32),
            pltpu.VMEM((share, topics), f32),
            pltpu.VMEM((1, topics), f32),
            pltpu.VMEM((share, topics), f32),
            pltpu.VMEM((2, CHAINS, docs, panel), bf16),
            pltpu.VMEM((CHAINS, docs, panel), bf16),
            pltpu.VMEM((panel, 2 * CHAINS * docs), bf16),
            pltpu.VMEM((2, panel, topics), bf16),
            pltpu.VMEM((ny, 2, CHAINS, sub, topics), bf16),
            pltpu.VMEM((CHAINS, sub, topics), f32),
            pltpu.VMEM((CHAINS, docs, topics), f32),
            pltpu.VMEM((CHAINS, ny, sub, topics), f32),
            pltpu.VMEM((nx, nz * share, topics), f32),
            pltpu.VMEM((nx, nz * share, topics), f32),
            pltpu.VMEM((nz, share, topics), f32),
            pltpu.VMEM((ny, 1, topics), f32),
            pltpu.VMEM((2, 1, topics), f32),
            pltpu.VMEM((nx, 1, topics), f32),
            pltpu.VMEM((nz, 1, topics), f32),
            dma((5,)), dma((ny,)), dma((2,)),
            dma((nz,)), dma((nz,)), dma((nx, nz)), dma((nx, nz)), dma((nx,)), dma((nx,)),
            dma((CHAINS, ny)), dma((CHAINS, ny)), dma((CHAINS, ny)), dma((CHAINS, ny)),
            dma((CHAINS,)), dma((CHAINS,)),
            dma((nx, nz)), dma((nx, nz)), dma((nz,)), dma((nz,)),
            dma((ny,)), dma((ny,)), dma, dma, dma((nx,)), dma((nx,)), dma((nz,)), dma((nz,)),
        ],
        compiler_params=pltpu.CompilerParams(
            collective_id=0, has_side_effects=True, vmem_limit_bytes=VMEM_LIMIT
        ),
    )(tile_doc, tile_word, tile_live, counts, doc_init, topic_word, topic_mass[None, :], noise)


def solution(mesh):
    return jax.shard_map(
        shards,
        mesh=mesh,
        in_specs=(
            P("dp", "vocab", None, None, None),
            P("dp", "vocab", None),
            P("dp", "vocab", None),
            P("dp", "vocab"),
            P("dp", None),
            P(("vocab", "dp"), None),
            P(),
            P(("vocab", "dp"), None),
        ),
        out_specs=(P(("dp", "vocab"), None), P(("vocab", "dp"), None)),
        check_vma=False,
    )
```

time: 147 us -> 137 us (0.932)
  Pallas kernels: 139 us -> 132 us
  local copies, waits for them, and re-layouts: 6.43 us -> 2.95 us
    pallas_call x1, Pallas kernels: 139 us -> 132 us  [shards(): pl.pallas_call(functools.partial(body, nx, nz, ny, share), out_shape=(jax...]
    unnamed x12 -> x2, local copies, waits for them, and re-layouts: 6.43 us -> 2.95 us
where the time goes in v2:
time: 137 us; the launch traced here: 136 us
  Pallas kernels  132 us (96%)
  local copies, waits for them, and re-layouts  2.95 us (2%)
    pallas_call x1, Pallas kernels, shards(): pl.pallas_call(functools.partial(body, nx, nz, ny, share), out_shape=(jax...  132 us
    unnamed x2, local copies, waits for them, and re-layouts  2.95 us

profile of v2, /device:TPU:1, one launch (start us, length us, event | category | flops | bytes accessed | tf_op | source)
XLA Modules:
  0.0 136.4 jit_solution(6964334074554267616)
XLA Ops:
  1.3 132.2 %shard_map.95 = (f32[32,512]{1,0:T(8,128)}, f32[32,512]{1,0:T(8,128)}) custom-call(s32[1,1,32]{2,1,0:T(1,128)} %doc_pick.1, s32[1,1,32]{2,1,0:T(1,128)} %word_pick.1, s32[1,1]{1,0:T(1,128)S(6)} %copy.12.live, s32[1,1,32,128,128]{4,3,2,1,0:T(8,128)} %counts_hbm.1, f32[512,512]{1,0:T(8,128)} %doc_hbm.1, f32[32,512]{1,0:T(8,128)} %word_hbm.1, ...), custom_call_target="tpu_custom_call" | custom-call | tf_op jit(solution)/shard_map/pallas_call | solution.py:408
  133.4 1.5 %copy.13 = f32[32,512]{1,0:T(8,128)} copy(f32[32,512]{1,0:T(8,128)} %get-tuple-element.4) | data formatting | bytes 131072
  134.9 1.5 %copy.14 = f32[32,512]{1,0:T(8,128)} copy(f32[32,512]{1,0:T(8,128)} %get-tuple-element.5) | data formatting | bytes 131072

commit v3 on v2

--- a/solution.py
+++ b/solution.py
@@ -14,6 +14,8 @@
 GRAD_SCALE = 16.0
 MESH = pl.DeviceIdType.MESH
 CHAINS = 2
+CODES = 65535.0
+SCALE_STEPS = 1024.0
 X_CHIPS = 4
 VMEM_LIMIT = 58 * 2**20
 
@@ -28,6 +30,30 @@
 
 def nt_dot(a, b):
     return lax.dot_general(a, b, (((1,), (1,)), ((), ())), preferred_element_type=jnp.float32)
+
+
+def pack(values):
+    half = values.shape[0] // 2
+    top = jnp.maximum(jnp.max(values, axis=0, keepdims=True), 1e-30)
+    scale = (jnp.log2(top) * SCALE_STEPS + 1.0).astype(jnp.int32)
+    factor = jnp.exp2(scale.astype(jnp.float32) * (-1.0 / SCALE_STEPS)) * CODES
+    code = jnp.minimum(values * factor + 0.5, CODES).astype(jnp.int32)
+    return code[:half] | (code[half:] << 16), scale
+
+
+def store_packed(ref, values):
+    half = values.shape[0] // 2
+    code, scale = pack(values)
+    ref[0:half, :] = code
+    ref[half:half + 1, :] = scale
+
+
+def unpack(ref):
+    half = ref.shape[0] - 1
+    code, scale = ref[0:half, :], ref[half:half + 1, :]
+    unit = jnp.exp2(scale.astype(jnp.float32) * (1.0 / SCALE_STEPS)) * (1.0 / CODES)
+    both = jnp.concatenate([code & 0xFFFF, (code >> 16) & 0xFFFF], axis=0)
+    return both.astype(jnp.float32) * unit
 
 
 def body(
@@ -35,7 +61,7 @@
     doc_pick, word_pick, live, counts_hbm, doc_hbm, word_hbm, mass_hbm, noise_hbm,
     doc_out, word_out,
     slot_vm, slot_ref, cbuf, dbuf, word_ref, mass_ref, noise_ref,
-    cnt, cnt_sib, cnt_t, prob, gall, gam, part, got, hits, got_x, got_z,
+    cnt, cnt_sib, cnt_t, prob, gall, gam, part, part_go, got, hits, hits_go, got_x, sum_go, got_z,
     tot_y, tot_c, tot_x, tot_z,
     in_sem, doc_sem, cnt_sem,
     pz_s, pz_r, px_s, px_r, pc_s, pc_r,
@@ -239,7 +265,13 @@
         return pl.ds(pl.multiple_of(lax.rem(y + j + ny, ny) * sub, sub), sub)
 
     def send_sums(h, j):
-        return remote(part.at[h, doc_rows(j)], got.at[h, j], s_s.at[h, j], s_r.at[h, j], at_y(j))
+        to = lax.rem(y + j, ny)
+        return remote(part_go.at[h, to], got.at[h, j], s_s.at[h, j], s_r.at[h, j], at_y(j))
+
+    def pack_sums(h):
+        for q in range(ny):
+            rows = slice(q * sub, (q + 1) * sub)
+            store_packed(part_go.at[h, q], part[h, rows, :] * gall[q, c, h].astype(jnp.float32))
 
     def send_gamma(h, j):
         own = gall.at[y, c, h]
@@ -257,13 +289,16 @@
                 for j in range(1, ny):
                     send_sums(h, j).wait_send()
                 partial_sums(h)
+            pack_sums(h)
             for j in far_first(ny):
                 send_sums(h, j).start()
         for h in range(CHAINS):
-            total = part[h, doc_rows(0), :]
+            total = None
             for j in near_first(ny):
                 send_sums(h, j).wait_recv()
-                total = total + got[h, j]
+                add = unpack(got.at[h, j])
+                total = add if total is None else total + add
+            total = part[h, doc_rows(0), :] + total / gall[y, c, h].astype(jnp.float32)
             gam[h] = ALPHA_PRIOR + gam[h] * total
             if it:
                 for j in range(1, ny):
@@ -309,12 +344,12 @@
 
     def send_hx(jx, jz):
         return remote(
-            hits.at[jx, z_rows(jz)], got_x.at[jx, z_rows(jz)],
+            hits_go.at[jx, lax.rem(z + jz, nz)], got_x.at[jx, jz],
             hx_s.at[jx, jz], hx_r.at[jx, jz], at_x(jx),
         )
 
     def send_hz(j):
-        return remote(hits.at[0, z_rows(j)], got_z.at[j], hz_s.at[j], hz_r.at[j], at_z(j))
+        return remote(sum_go.at[j], got_z.at[j], hz_s.at[j], hz_r.at[j], at_z(j))
 
     def send_tx(j):
         return remote(tot_x.at[0], tot_x.at[j], tx_s.at[j], tx_r.at[j], at_x(j))
@@ -326,10 +361,14 @@
     z_order = far_first(nz) + [0]
     for jx in far_first(nx) + [0]:
         words = word_block(nx - jx)
-        rates = nt_dot(prob[c, words, :], gamma_all)
-        ratios = (cnt_t[words, :].astype(jnp.float32) / rates).astype(jnp.bfloat16)
-        hits[jx] = jnp.dot(ratios, gamma_all, preferred_element_type=jnp.float32)
-        if jx:
+        p = prob[c, words, :]
+        ratios = (cnt_t[words, :].astype(jnp.float32) / nt_dot(p, gamma_all)).astype(jnp.bfloat16)
+        found = jnp.dot(ratios, gamma_all, preferred_element_type=jnp.float32) * p.astype(jnp.float32)
+        if not jx:
+            hits[...] = found
+        else:
+            for q in range(nz):
+                store_packed(hits_go.at[jx, q], found[q * share:(q + 1) * share])
             for jz in z_order:
                 send_hx(jx, jz).start()
 
@@ -346,26 +385,27 @@
         send_tz(j).start()
 
     for jz in z_order:
-        total = hits[0, z_rows(jz), :]
+        total = hits[z_rows(jz), :]
         for jx in range(1, nx):
             send_hx(jx, jz).wait_recv()
-            total = total + got_x[jx, z_rows(jz), :]
-        hits[0, z_rows(jz), :] = total
+            total = total + unpack(got_x.at[jx, jz])
         if jz:
+            store_packed(sum_go.at[jz], total)
             send_hz(jz).start()
+    reduced = total
 
     totals = tot_z[0]
     for j in near_first(nz):
         send_tz(j).wait_recv()
         totals = totals + tot_z[j]
     noise_in.wait()
-    reduced = hits[0, z_rows(0), :]
     for j in near_first(nz):
         send_hz(j).wait_recv()
-        reduced = reduced + got_z[j]
+        reduced = reduced + unpack(got_z.at[j])
     word = word_ref[...]
     probs = word / mass_ref[...]
-    drift = BETA_PRIOR - word + GRAD_SCALE * (probs * reduced - totals * probs)
+    counted = reduced * (probs / prob[c, word_rows(0, 0), :].astype(jnp.float32))
+    drift = BETA_PRIOR - word + GRAD_SCALE * (counted - totals * probs)
     word_out[...] = jnp.abs(word + HALF_STEP * drift + jnp.sqrt(word) * noise_ref[...])
 
     for j in range(1, nz):
@@ -401,7 +441,7 @@
     sub = share // CHAINS
     docs = ny * sub
 
-    f32, bf16, dma = jnp.float32, jnp.bfloat16, pltpu.SemaphoreType.DMA
+    f32, bf16, i32, dma = jnp.float32, jnp.bfloat16, jnp.int32, pltpu.SemaphoreType.DMA
     vmem = pl.BlockSpec(memory_space=pltpu.VMEM)
     smem = pl.BlockSpec(memory_space=pltpu.SMEM)
     hbm = pl.BlockSpec(memory_space=pl.ANY)
@@ -428,10 +468,13 @@
             pltpu.VMEM((ny, 2, CHAINS, sub, topics), bf16),
             pltpu.VMEM((CHAINS, sub, topics), f32),
             pltpu.VMEM((CHAINS, docs, topics), f32),
-            pltpu.VMEM((CHAINS, ny, sub, topics), f32),
-            pltpu.VMEM((nx, nz * share, topics), f32),
-            pltpu.VMEM((nx, nz * share, topics), f32),
-            pltpu.VMEM((nz, share, topics), f32),
+            pltpu.VMEM((CHAINS, ny, sub // 2 + 1, topics), i32),
+            pltpu.VMEM((CHAINS, ny, sub // 2 + 1, topics), i32),
+            pltpu.VMEM((nz * share, topics), f32),
+            pltpu.VMEM((nx, nz, share // 2 + 1, topics), i32),
+            pltpu.VMEM((nx, nz, share // 2 + 1, topics), i32),
+            pltpu.VMEM((nz, share // 2 + 1, topics), i32),
+            pltpu.VMEM((nz, share // 2 + 1, topics), i32),
             pltpu.VMEM((ny, 1, topics), f32),
             pltpu.VMEM((2, 1, topics), f32),
             pltpu.VMEM((nx, 1, topics), f32),

time: 137 us -> 129 us (0.942)
  Pallas kernels: 132 us -> 125 us
    pallas_call x1, Pallas kernels: 132 us -> 125 us  [shards(): pl.pallas_call(functools.partial(body, nx, nz, ny, share), out_shape=(jax...]
where the time goes in v3:
time: 129 us
  Pallas kernels  125 us (97%)
  local copies, waits for them, and re-layouts  2.95 us (2%)
  between operations  1.29 us (1%)
    pallas_call x1, Pallas kernels, shards(): pl.pallas_call(functools.partial(body, nx, nz, ny, share), out_shape=(jax...  125 us
    unnamed x2, local copies, waits for them, and re-layouts  2.95 us

profile of v3, /device:TPU:1, one launch (start us, length us, event | category | flops | bytes accessed | tf_op | source)
XLA Modules:
  0.0 129.1 jit_solution(6423271972037128202)
XLA Ops:
  1.3 124.9 %shard_map.95 = (f32[32,512]{1,0:T(8,128)}, f32[32,512]{1,0:T(8,128)}) custom-call(s32[1,1,32]{2,1,0:T(1,128)} %doc_pick.1, s32[1,1,32]{2,1,0:T(1,128)} %word_pick.1, s32[1,1]{1,0:T(1,128)S(6)} %copy.12.live, s32[1,1,32,128,128]{4,3,2,1,0:T(8,128)} %counts_hbm.1, f32[512,512]{1,0:T(8,128)} %doc_hbm.1, f32[32,512]{1,0:T(8,128)} %word_hbm.1, ...), custom_call_target="tpu_custom_call" | custom-call | tf_op jit(solution)/shard_map/pallas_call | solution.py:448
  126.1 1.5 %copy.13 = f32[32,512]{1,0:T(8,128)} copy(f32[32,512]{1,0:T(8,128)} %get-tuple-element.4) | data formatting | bytes 131072
  127.6 1.5 %copy.14 = f32[32,512]{1,0:T(8,128)} copy(f32[32,512]{1,0:T(8,128)} %get-tuple-element.5) | data formatting | bytes 131072

commit v4 on v3

--- a/solution.py
+++ b/solution.py
@@ -41,17 +41,13 @@
     return code[:half] | (code[half:] << 16), scale
 
 
-def store_packed(ref, values):
-    half = values.shape[0] // 2
-    code, scale = pack(values)
-    ref[0:half, :] = code
-    ref[half:half + 1, :] = scale
-
-
-def unpack(ref):
-    half = ref.shape[0] - 1
-    code, scale = ref[0:half, :], ref[half:half + 1, :]
-    unit = jnp.exp2(scale.astype(jnp.float32) * (1.0 / SCALE_STEPS)) * (1.0 / CODES)
+def store_packed(ref, scale_ref, values):
+    ref[...], scale_ref[...] = pack(values)
+
+
+def unpack(ref, scale_ref):
+    code = ref[...]
+    unit = jnp.exp2(scale_ref[...].astype(jnp.float32) * (1.0 / SCALE_STEPS)) * (1.0 / CODES)
     both = jnp.concatenate([code & 0xFFFF, (code >> 16) & 0xFFFF], axis=0)
     return both.astype(jnp.float32) * unit
 
@@ -61,12 +57,13 @@
     doc_pick, word_pick, live, counts_hbm, doc_hbm, word_hbm, mass_hbm, noise_hbm,
     doc_out, word_out,
     slot_vm, slot_ref, cbuf, dbuf, word_ref, mass_ref, noise_ref,
-    cnt, cnt_sib, cnt_t, prob, gall, gam, part, part_go, got, hits, hits_go, got_x, sum_go, got_z,
+    cnt, cnt_sib, cnt_t, prob, gall, gam, part, part_go, part_sc, got, got_sc,
+    hits, hits_go, hits_sc, got_x, got_xs, sum_go, sum_sc, got_z, got_zs,
     tot_y, tot_c, tot_x, tot_z,
     in_sem, doc_sem, cnt_sem,
     pz_s, pz_r, px_s, px_r, pc_s, pc_r,
-    s_s, s_r, g_s, g_r, gc_s, gc_r,
-    hx_s, hx_r, hz_s, hz_r,
+    s_s, s_r, sc_s, sc_r, g_s, g_r, gc_s, gc_r,
+    hx_s, hx_r, xs_s, xs_r, hz_s, hz_r, zs_s, zs_r,
     ty_s, ty_r, tc_s, tc_r, tx_s, tx_r, tz_s, tz_r,
 ):
     slots, block = counts_hbm.shape[2], counts_hbm.shape[3]
@@ -268,10 +265,15 @@
         to = lax.rem(y + j, ny)
         return remote(part_go.at[h, to], got.at[h, j], s_s.at[h, j], s_r.at[h, j], at_y(j))
 
+    def send_scale(h, j):
+        to = lax.rem(y + j, ny)
+        return remote(part_sc.at[h, to], got_sc.at[h, j], sc_s.at[h, j], sc_r.at[h, j], at_y(j))
+
     def pack_sums(h):
         for q in range(ny):
             rows = slice(q * sub, (q + 1) * sub)
-            store_packed(part_go.at[h, q], part[h, rows, :] * gall[q, c, h].astype(jnp.float32))
+            here = part[h, rows, :] * gall[q, c, h].astype(jnp.float32)
+            store_packed(part_go.at[h, q], part_sc.at[h, q], here)
 
     def send_gamma(h, j):
         own = gall.at[y, c, h]
@@ -288,15 +290,18 @@
                     wait_gamma(h, j)
                 for j in range(1, ny):
                     send_sums(h, j).wait_send()
+                    send_scale(h, j).wait_send()
                 partial_sums(h)
             pack_sums(h)
             for j in far_first(ny):
+                send_scale(h, j).start()
                 send_sums(h, j).start()
         for h in range(CHAINS):
             total = None
             for j in near_first(ny):
+                send_scale(h, j).wait_recv()
                 send_sums(h, j).wait_recv()
-                add = unpack(got.at[h, j])
+                add = unpack(got.at[h, j], got_sc.at[h, j])
                 total = add if total is None else total + add
             total = part[h, doc_rows(0), :] + total / gall[y, c, h].astype(jnp.float32)
             gam[h] = ALPHA_PRIOR + gam[h] * total
@@ -348,6 +353,12 @@
             hx_s.at[jx, jz], hx_r.at[jx, jz], at_x(jx),
         )
 
+    def send_xs(jx):
+        return remote(hits_sc.at[jx], got_xs.at[jx], xs_s.at[jx], xs_r.at[jx], at_x(jx))
+
+    def send_zs(j):
+        return remote(sum_sc.at[j], got_zs.at[j], zs_s.at[j], zs_r.at[j], at_z(j))
+
     def send_hz(j):
         return remote(sum_go.at[j], got_z.at[j], hz_s.at[j], hz_r.at[j], at_z(j))
 
@@ -368,7 +379,8 @@
             hits[...] = found
         else:
             for q in range(nz):
-                store_packed(hits_go.at[jx, q], found[q * share:(q + 1) * share])
+                store_packed(hits_go.at[jx, q], hits_sc.at[jx, q], found[q * share:(q + 1) * share])
+            send_xs(jx).start()
             for jz in z_order:
                 send_hx(jx, jz).start()
 
@@ -384,13 +396,16 @@
     for j in far_first(nz):
         send_tz(j).start()
 
+    for jx in far_first(nx):
+        send_xs(jx).wait_recv()
     for jz in z_order:
         total = hits[z_rows(jz), :]
         for jx in range(1, nx):
             send_hx(jx, jz).wait_recv()
-            total = total + unpack(got_x.at[jx, jz])
+            total = total + unpack(got_x.at[jx, jz], got_xs.at[jx, lax.rem(z + jz, nz)])
         if jz:
-            store_packed(sum_go.at[jz], total)
+            store_packed(sum_go.at[jz], sum_sc.at[jz], total)
+            send_zs(jz).start()
             send_hz(jz).start()
     reduced = total
 
@@ -400,8 +415,9 @@
         totals = totals + tot_z[j]
     noise_in.wait()
     for j in near_first(nz):
+        send_zs(j).wait_recv()
         send_hz(j).wait_recv()
-        reduced = reduced + unpack(got_z.at[j])
+        reduced = reduced + unpack(got_z.at[j], got_zs.at[j])
     word = word_ref[...]
     probs = word / mass_ref[...]
     counted = reduced * (probs / prob[c, word_rows(0, 0), :].astype(jnp.float32))
@@ -411,9 +427,11 @@
     for j in range(1, nz):
         pz[j].wait_send()
         send_hz(j).wait_send()
+        send_zs(j).wait_send()
         send_tz(j).wait_send()
     for jx in range(1, nx):
         send_tx(jx).wait_send()
+        send_xs(jx).wait_send()
         for jz in range(nz):
             px[jx, jz].wait_send()
             send_hx(jx, jz).wait_send()
@@ -425,6 +443,7 @@
         give(h).wait_send()
         for j in range(1, ny):
             send_sums(h, j).wait_send()
+            send_scale(h, j).wait_send()
             send_gamma(h, j).wait_send()
     for j in range(1, ny):
         send_ty(j).wait_send()
@@ -468,13 +487,19 @@
             pltpu.VMEM((ny, 2, CHAINS, sub, topics), bf16),
             pltpu.VMEM((CHAINS, sub, topics), f32),
             pltpu.VMEM((CHAINS, docs, topics), f32),
-            pltpu.VMEM((CHAINS, ny, sub // 2 + 1, topics), i32),
-            pltpu.VMEM((CHAINS, ny, sub // 2 + 1, topics), i32),
+            pltpu.VMEM((CHAINS, ny, sub // 2, topics), i32),
+            pltpu.VMEM((CHAINS, ny, 1, topics), i32),
+            pltpu.VMEM((CHAINS, ny, sub // 2, topics), i32),
+            pltpu.VMEM((CHAINS, ny, 1, topics), i32),
             pltpu.VMEM((nz * share, topics), f32),
-            pltpu.VMEM((nx, nz, share // 2 + 1, topics), i32),
-            pltpu.VMEM((nx, nz, share // 2 + 1, topics), i32),
-            pltpu.VMEM((nz, share // 2 + 1, topics), i32),
-            pltpu.VMEM((nz, share // 2 + 1, topics), i32),
+            pltpu.VMEM((nx, nz, share // 2, topics), i32),
+            pltpu.VMEM((nx, nz, 1, topics), i32),
+            pltpu.VMEM((nx, nz, share // 2, topics), i32),
+            pltpu.VMEM((nx, nz, 1, topics), i32),
+            pltpu.VMEM((nz, share // 2, topics), i32),
+            pltpu.VMEM((nz, 1, topics), i32),
+            pltpu.VMEM((nz, share // 2, topics), i32),
+            pltpu.VMEM((nz, 1, topics), i32),
             pltpu.VMEM((ny, 1, topics), f32),
             pltpu.VMEM((2, 1, topics), f32),
             pltpu.VMEM((nx, 1, topics), f32),
@@ -482,8 +507,10 @@
             dma((5,)), dma((ny,)), dma((2,)),
             dma((nz,)), dma((nz,)), dma((nx, nz)), dma((nx, nz)), dma((nx,)), dma((nx,)),
             dma((CHAINS, ny)), dma((CHAINS, ny)), dma((CHAINS, ny)), dma((CHAINS, ny)),
+            dma((CHAINS, ny)), dma((CHAINS, ny)),
             dma((CHAINS,)), dma((CHAINS,)),
-            dma((nx, nz)), dma((nx, nz)), dma((nz,)), dma((nz,)),
+            dma((nx, nz)), dma((nx, nz)), dma((nx,)), dma((nx,)),
+            dma((nz,)), dma((nz,)), dma((nz,)), dma((nz,)),
             dma((ny,)), dma((ny,)), dma, dma, dma((nx,)), dma((nx,)), dma((nz,)), dma((nz,)),
         ],
         compiler_params=pltpu.CompilerParams(

time: 129 us -> 108 us (0.84)
  Pallas kernels: 125 us -> 104 us
    pallas_call x1, Pallas kernels: 125 us -> 104 us  [shards(): pl.pallas_call(functools.partial(body, nx, nz, ny, share), out_shape=(jax...]
where the time goes in v4:
time: 108 us
  Pallas kernels  104 us (96%)
  local copies, waits for them, and re-layouts  2.95 us (3%)
  between operations  1.29 us (1%)
    pallas_call x1, Pallas kernels, shards(): pl.pallas_call(functools.partial(body, nx, nz, ny, share), out_shape=(jax...  104 us
    unnamed x2, local copies, waits for them, and re-layouts  2.95 us

profile of v4, /device:TPU:1, one launch (start us, length us, event | category | flops | bytes accessed | tf_op | source)
XLA Modules:
  0.0 108.1 jit_solution(15459699919780468708)
XLA Ops:
  1.3 103.9 %shard_map.95 = (f32[32,512]{1,0:T(8,128)}, f32[32,512]{1,0:T(8,128)}) custom-call(s32[1,1,32]{2,1,0:T(1,128)} %doc_pick.1, s32[1,1,32]{2,1,0:T(1,128)} %word_pick.1, s32[1,1]{1,0:T(1,128)S(6)} %copy.12.live, s32[1,1,32,128,128]{4,3,2,1,0:T(8,128)} %counts_hbm.1, f32[512,512]{1,0:T(8,128)} %doc_hbm.1, f32[32,512]{1,0:T(8,128)} %word_hbm.1, ...), custom_call_target="tpu_custom_call" | custom-call | tf_op jit(solution)/shard_map/pallas_call | solution.py:467
  105.2 1.5 %copy.13 = f32[32,512]{1,0:T(8,128)} copy(f32[32,512]{1,0:T(8,128)} %get-tuple-element.4) | data formatting | bytes 131072
  106.7 1.5 %copy.14 = f32[32,512]{1,0:T(8,128)} copy(f32[32,512]{1,0:T(8,128)} %get-tuple-element.5) | data formatting | bytes 131072

commit v5 on v4

--- a/solution.py
+++ b/solution.py
@@ -54,9 +54,9 @@
 
 def body(
     nx, nz, ny, share,
-    doc_pick, word_pick, live, counts_hbm, doc_hbm, word_hbm, mass_hbm, noise_hbm,
+    doc_table, word_table, live_table, counts_hbm, doc_hbm, word_hbm, mass_hbm, noise_hbm,
     doc_out, word_out,
-    slot_vm, slot_ref, cbuf, dbuf, word_ref, mass_ref, noise_ref,
+    doc_pick, word_pick, live, slot_vm, slot_ref, cbuf, dbuf, word_ref, mass_ref, noise_ref,
     cnt, cnt_sib, cnt_t, prob, gall, gam, part, part_go, part_sc, got, got_sc,
     hits, hits_go, hits_sc, got_x, got_xs, sum_go, sum_sc, got_z, got_zs,
     tot_y, tot_c, tot_x, tot_z,
@@ -105,6 +105,14 @@
     for to in peers:
         pl.semaphore_signal(barrier, inc=1, device_id=to, device_id_type=MESH)
 
+    tables = [
+        pltpu.make_async_copy(src, dst, in_sem.at[5 + i])
+        for i, (src, dst) in enumerate(
+            ((doc_table, doc_pick), (word_table, word_pick), (live_table, live))
+        )
+    ]
+    for copy in tables:
+        copy.start()
     counts_in = pltpu.make_async_copy(counts_hbm.at[0, 0], cbuf.at[pl.ds(0, slots)], in_sem.at[2])
     counts_in.start()
     doc_in = [
@@ -117,16 +125,6 @@
         copy.start()
     noise_in = pltpu.make_async_copy(noise_hbm, noise_ref, in_sem.at[3])
     noise_in.start()
-
-    lane = lax.broadcasted_iota(jnp.int32, (1, 128), 1)
-    slot_of = jnp.full((1, 128), slots, jnp.int32)
-    for s in range(slots):
-        key = doc_pick[0, 0, s] * wblocks + word_pick[0, 0, s]
-        use = jnp.where(s < live[0, 0], s, slots)
-        slot_of = jnp.where(lane == key, use, slot_of)
-    slot_vm[...] = slot_of
-    slot_in = pltpu.make_async_copy(slot_vm, slot_ref, in_sem.at[4])
-    slot_in.start()
 
     def word_rows(jx, jz):
         row = (lax.rem(x - jx + nx, nx) * nz + lax.rem(z - jz + nz, nz)) * share
@@ -157,6 +155,18 @@
         pz[j].start()
     for jx in far_first(nx):
         px[jx, 0].start()
+
+    for copy in tables:
+        copy.wait()
+    lane = lax.broadcasted_iota(jnp.int32, (1, 128), 1)
+    slot_of = jnp.full((1, 128), slots, jnp.int32)
+    for s in range(slots):
+        key = doc_pick[0, 0, s] * wblocks + word_pick[0, 0, s]
+        use = jnp.where(s < live[0, 0], s, slots)
+        slot_of = jnp.where(lane == key, use, slot_of)
+    slot_vm[...] = slot_of
+    slot_in = pltpu.make_async_copy(slot_vm, slot_ref, in_sem.at[4])
+    slot_in.start()
 
     for copy in doc_in:
         copy.wait()
@@ -368,9 +378,14 @@
     def send_tz(j):
         return remote(tot_z.at[0], tot_z.at[j], tz_s.at[j], tz_r.at[j], at_z(j))
 
+    send_tc.wait_recv()
+    tot_x[0] = tot_c[0] + tot_c[1]
+    for j in far_first(nx):
+        send_tx(j).start()
     gamma_all = gall[...].reshape(2 * CHAINS * docs, topics)
-    z_order = far_first(nz) + [0]
-    for jx in far_first(nx) + [0]:
+    z_order, x_order = far_first(nz) + [0], far_first(nx)
+    early = nz // 2
+    for jx in x_order + [0]:
         words = word_block(nx - jx)
         p = prob[c, words, :]
         ratios = (cnt_t[words, :].astype(jnp.float32) / nt_dot(p, gamma_all)).astype(jnp.bfloat16)
@@ -381,13 +396,15 @@
             for q in range(nz):
                 store_packed(hits_go.at[jx, q], hits_sc.at[jx, q], found[q * share:(q + 1) * share])
             send_xs(jx).start()
-            for jz in z_order:
-                send_hx(jx, jz).start()
-
-    send_tc.wait_recv()
-    tot_x[0] = tot_c[0] + tot_c[1]
-    for j in far_first(nx):
-        send_tx(j).start()
+            if jx == x_order[0]:
+                for jz in z_order[:early]:
+                    send_hx(jx, jz).start()
+            if jx == x_order[-1]:
+                for jz in z_order:
+                    for to in x_order:
+                        if to != x_order[0] or jz not in z_order[:early]:
+                            send_hx(to, jz).start()
+
     total = tot_x[0]
     for j in near_first(nx):
         send_tx(j).wait_recv()
@@ -462,7 +479,6 @@
 
     f32, bf16, i32, dma = jnp.float32, jnp.bfloat16, jnp.int32, pltpu.SemaphoreType.DMA
     vmem = pl.BlockSpec(memory_space=pltpu.VMEM)
-    smem = pl.BlockSpec(memory_space=pltpu.SMEM)
     hbm = pl.BlockSpec(memory_space=pl.ANY)
     return pl.pallas_call(
         functools.partial(body, nx, nz, ny, share),
@@ -470,9 +486,12 @@
             jax.ShapeDtypeStruct((share, topics), f32),
             jax.ShapeDtypeStruct((share, topics), f32),
         ),
-        in_specs=[smem, smem, smem, hbm, hbm, hbm, hbm, hbm],
+        in_specs=[hbm, hbm, hbm, hbm, hbm, hbm, hbm, hbm],
         out_specs=(vmem, vmem),
         scratch_shapes=[
+            pltpu.SMEM((1, 1, slots), i32),
+            pltpu.SMEM((1, 1, slots), i32),
+            pltpu.SMEM((1, 1), i32),
             pltpu.VMEM((1, 128), jnp.int32),
             pltpu.SMEM((1, 128), jnp.int32),
             pltpu.VMEM((slots + 1, block, block), jnp.int32),
@@ -504,7 +523,7 @@
             pltpu.VMEM((2, 1, topics), f32),
             pltpu.VMEM((nx, 1, topics), f32),
             pltpu.VMEM((nz, 1, topics), f32),
-            dma((5,)), dma((ny,)), dma((2,)),
+            dma((8,)), dma((ny,)), dma((2,)),
             dma((nz,)), dma((nz,)), dma((nx, nz)), dma((nx, nz)), dma((nx,)), dma((nx,)),
             dma((CHAINS, ny)), dma((CHAINS, ny)), dma((CHAINS, ny)), dma((CHAINS, ny)),
             dma((CHAINS, ny)), dma((CHAINS, ny)),

time: 108 us -> 102 us (0.944)
  Pallas kernels: 104 us -> 97.1 us
    pallas_call x1, Pallas kernels: 104 us -> 97.1 us  [shards(): pl.pallas_call(functools.partial(body, nx, nz, ny, share), out_shape=(jax...]
where the time goes in v5:
time: 102 us; the launch traced here: 101 us
  Pallas kernels  97.1 us (95%)
  local copies, waits for them, and re-layouts  2.95 us (3%)
  between operations  1.29 us (1%)
    pallas_call x1, Pallas kernels, shards(): pl.pallas_call(functools.partial(body, nx, nz, ny, share), out_shape=(jax...  97.1 us
    unnamed x2, local copies, waits for them, and re-layouts  2.95 us

profile of v5, /device:TPU:1, one launch (start us, length us, event | category | flops | bytes accessed | tf_op | source)
XLA Modules:
  0.0 101.4 jit_solution(11057316649227078754)
XLA Ops:
  1.3 97.1 %shard_map.95 = (f32[32,512]{1,0:T(8,128)}, f32[32,512]{1,0:T(8,128)}) custom-call(s32[1,1,32]{2,1,0:T(1,128)} %doc_table.1, s32[1,1,32]{2,1,0:T(1,128)} %word_table.1, s32[1,1]{1,0:T(1,128)S(6)} %copy.12.live_table, s32[1,1,32,128,128]{4,3,2,1,0:T(8,128)} %counts_hbm.1, f32[512,512]{1,0:T(8,128)} %doc_hbm.1, f32[32,512]{1,0:T(8,128)} %word_hbm.1, ...), custom_call_target="tpu_custom_call" | custom-call | tf_op jit(solution)/shard_map/pallas_call | solution.py:483
  98.4 1.5 %copy.13 = f32[32,512]{1,0:T(8,128)} copy(f32[32,512]{1,0:T(8,128)} %get-tuple-element.4) | data formatting | bytes 131072
  99.9 1.5 %copy.14 = f32[32,512]{1,0:T(8,128)} copy(f32[32,512]{1,0:T(8,128)} %get-tuple-element.5) | data formatting | bytes 131072

commit v6 on v5

--- a/solution.py
+++ b/solution.py
@@ -305,6 +305,7 @@
             pack_sums(h)
             for j in far_first(ny):
                 send_scale(h, j).start()
+            for j in far_first(ny):
                 send_sums(h, j).start()
         for h in range(CHAINS):
             total = None

time: 102 us -> 101 us (level)
  no operation moved by 1% of the time
where the time goes in v6:
time: 101 us; the launch traced here: 100 us
  Pallas kernels  96.1 us (95%)
  local copies, waits for them, and re-layouts  2.95 us (3%)
  between operations  1.29 us (1%)
    pallas_call x1, Pallas kernels, shards(): pl.pallas_call(functools.partial(body, nx, nz, ny, share), out_shape=(jax...  96.1 us
    unnamed x2, local copies, waits for them, and re-layouts  2.95 us

profile of v6, /device:TPU:1, one launch (start us, length us, event | category | flops | bytes accessed | tf_op | source)
XLA Modules:
  0.0 100.4 jit_solution(11611513687627520308)
XLA Ops:
  1.3 96.1 %shard_map.95 = (f32[32,512]{1,0:T(8,128)}, f32[32,512]{1,0:T(8,128)}) custom-call(s32[1,1,32]{2,1,0:T(1,128)} %doc_table.1, s32[1,1,32]{2,1,0:T(1,128)} %word_table.1, s32[1,1]{1,0:T(1,128)S(6)} %copy.12.live_table, s32[1,1,32,128,128]{4,3,2,1,0:T(8,128)} %counts_hbm.1, f32[512,512]{1,0:T(8,128)} %doc_hbm.1, f32[32,512]{1,0:T(8,128)} %word_hbm.1, ...), custom_call_target="tpu_custom_call" | custom-call | tf_op jit(solution)/shard_map/pallas_call | solution.py:484
  97.4 1.5 %copy.13 = f32[32,512]{1,0:T(8,128)} copy(f32[32,512]{1,0:T(8,128)} %get-tuple-element.4) | data formatting | bytes 131072
  98.9 1.5 %copy.14 = f32[32,512]{1,0:T(8,128)} copy(f32[32,512]{1,0:T(8,128)} %get-tuple-element.5) | data formatting | bytes 131072

commit v7 on v6

--- a/solution.py
+++ b/solution.py
@@ -309,7 +309,7 @@
                 send_sums(h, j).start()
         for h in range(CHAINS):
             total = None
-            for j in near_first(ny):
+            for j in far_first(ny):
                 send_scale(h, j).wait_recv()
                 send_sums(h, j).wait_recv()
                 add = unpack(got.at[h, j], got_sc.at[h, j])
@@ -432,7 +432,7 @@
         send_tz(j).wait_recv()
         totals = totals + tot_z[j]
     noise_in.wait()
-    for j in near_first(nz):
+    for j in far_first(nz):
         send_zs(j).wait_recv()
         send_hz(j).wait_recv()
         reduced = reduced + unpack(got_z.at[j], got_zs.at[j])

time: 101 us -> 101 us (level)
  no operation moved by 1% of the time
where the time goes in v7:
time: 101 us; the launch traced here: 100 us
  Pallas kernels  96.2 us (95%)
  local copies, waits for them, and re-layouts  2.95 us (3%)
  between operations  1.29 us (1%)
    pallas_call x1, Pallas kernels, shards(): pl.pallas_call(functools.partial(body, nx, nz, ny, share), out_shape=(jax...  96.2 us
    unnamed x2, local copies, waits for them, and re-layouts  2.95 us

profile of v7, /device:TPU:1, one launch (start us, length us, event | category | flops | bytes accessed | tf_op | source)
XLA Modules:
  0.0 100.4 jit_solution(286851522253407023)
XLA Ops:
  1.3 96.2 %shard_map.95 = (f32[32,512]{1,0:T(8,128)}, f32[32,512]{1,0:T(8,128)}) custom-call(s32[1,1,32]{2,1,0:T(1,128)} %doc_table.1, s32[1,1,32]{2,1,0:T(1,128)} %word_table.1, s32[1,1]{1,0:T(1,128)S(6)} %copy.12.live_table, s32[1,1,32,128,128]{4,3,2,1,0:T(8,128)} %counts_hbm.1, f32[512,512]{1,0:T(8,128)} %doc_hbm.1, f32[32,512]{1,0:T(8,128)} %word_hbm.1, ...), custom_call_target="tpu_custom_call" | custom-call | tf_op jit(solution)/shard_map/pallas_call | solution.py:484
  97.4 1.5 %copy.13 = f32[32,512]{1,0:T(8,128)} copy(f32[32,512]{1,0:T(8,128)} %get-tuple-element.4) | data formatting | bytes 131072
  98.9 1.5 %copy.14 = f32[32,512]{1,0:T(8,128)} copy(f32[32,512]{1,0:T(8,128)} %get-tuple-element.5) | data formatting | bytes 131072
